TPU v7x, 32 devices: a whole 2x2x4 slice. The times are simulated.
32 devices in a mesh: groups: 2 (over y), date: 4 (over z), rng: 2 (over x), az: 2 (over core).
Axes of the slice: x: 2, y: 2, z: 4, core: 2. Of those that a mesh axis runs over, the one named last changes fastest.
Arguments:
- slc: bfloat16 [2, 8, 64, 5120], P(None, ('groups', 'date'), 'az', 'rng'), parts along dimension 1, may hold values from -24 to 24
- offsets: int32 [8, 2], P(('groups', 'date')), parts along dimension 0, may hold values from -24 to 24, as said below
- kernel_index: int32 [8, 2], P(('groups', 'date')), parts along dimension 0, may hold values from 0 to 15
- range_shift: float32 [8], P('groups'), parts along dimension 0, may hold values from -0.15 to 0.15
Outputs:
- ifg: float32 [2, 8, 8, 16, 256], P(None, ('groups', 'date'), None, 'az', 'rng'), parts along dimension 1
There are 2 independent parts, one for each index of `groups`. A program takes and returns all parts, laid end to end along the dimension named above; each array names one. Nothing has to cross between parts.
Inputs may be any that keep to these rules, and one draw needn't show every extreme that they name: `offsets`: column 0 is the azimuth offset, within -8 to 8; column 1 is the range offset. Both ends of both ranges are taken by some date.
All inputs are finite; a program needn't handle non-finite values.
Results may differ from a plain program's by a relative error of at most 0.0039.
Values may be sent and summed in bfloat16 or wider, within the bound.
No kernel may reach another device: no remote copies, remote signals or barrier semaphores. Data moves between devices by JAX's collectives and lax.ppermute only.
A program may use at most 64 MiB of HBM per device.

v0:
```python
import functools

import jax
import jax.numpy as jnp
import numpy as np
from jax import lax
from jax.experimental import pallas as pl
from jax.experimental.pallas import tpu as pltpu
from jax.sharding import PartitionSpec as P

LAGS = 8
KERNELS = 16
TAPS = 8
FILTER_HALF = 8
FILTER_TAPS = 2 * FILTER_HALF + 1
LOOK_AZ = 4
LOOK_RG = 20
LANES = 128
META = 3
UNROLLED_PAIRS = 12


def up(value, unit):
    return -(-value // unit) * unit


def kernel_table():
    position = np.arange(TAPS) - 3.0 - np.arange(KERNELS)[:, None] / KERNELS
    shaped = np.sinc(position) * (0.5 + 0.5 * np.cos(np.pi * position / 5.0))
    table = np.zeros((KERNELS, LANES), np.float32)
    table[:, :TAPS] = shaped / shaped.sum(1, keepdims=True)
    return table


def lowpass_row(width):
    t = np.arange(FILTER_TAPS) - FILTER_HALF
    row = np.zeros((1, width), np.float32)
    row[0, :FILTER_TAPS] = 0.4 * np.sinc(0.4 * t) * (0.54 + 0.46 * np.cos(np.pi * t / (FILTER_HALF + 1)))
    return row


def halves(value):
    high = value.astype(jnp.bfloat16)
    return high, (value - high.astype(jnp.float32)).astype(jnp.bfloat16)


def dot(a, b):
    return jnp.dot(a, b, preferred_element_type=jnp.float32)


def dot_nt(a, b):
    return lax.dot_general(a, b, (((1,), (1,)), ((), ())), preferred_element_type=jnp.float32)


def pack_kernel(chunk, place_ref, offsets_ref, index_ref, slc_ref, before_ref, after_ref, out_ref, wide_ref):
    columns = slc_ref.shape[1]
    wide = out_ref.shape[2]
    first = place_ref[0] == 0
    last = place_ref[0] == place_ref[1] - 1
    zero = jnp.zeros_like(before_ref[...])
    wide_ref[:, :LANES] = jnp.where(first, zero, before_ref[...])
    wide_ref[:, LANES : LANES + columns] = slc_ref[...]
    wide_ref[:, LANES + columns :] = jnp.where(last, zero, after_ref[...])
    lane = lax.broadcasted_iota(jnp.int32, (slc_ref.shape[0], wide), 1)
    numbers = [offsets_ref[0, 0], index_ref[0, 0], index_ref[0, 1]]
    for j in range(out_ref.shape[0]):
        start = LANES + chunk * j - FILTER_HALF - 3 + offsets_ref[0, 1]
        tile = lax.shift_right_logical(start, 7)
        within = lax.bitwise_and(start, LANES - 1)
        window = wide_ref[:, pl.ds(pl.multiple_of(tile * LANES, LANES), wide + LANES)].astype(jnp.float32)
        moved = pltpu.roll(window, wide + LANES - within, 1)[:, :wide]
        for slot, number in enumerate(numbers):
            moved = jnp.where(lane == wide - META + slot, number.astype(jnp.float32), moved)
        out_ref[j] = moved.astype(jnp.bfloat16)


def picked_taps(table, index):
    row = lax.broadcasted_iota(jnp.int32, table.shape, 0).astype(jnp.float32)
    return jnp.sum(jnp.where(row == index, table, 0.0), axis=0, keepdims=True)


def banded(taps, distance):
    out = jnp.zeros(distance.shape, jnp.float32)
    for q in range(TAPS):
        out = jnp.where(distance == q, taps[:, q : q + 1], out)
    return out


def pairs_kernel(chunk, pairs, *refs):
    if isinstance(pairs, int):
        table_of_pairs, refs = refs[0], refs[1:]
    shift_ref, table_ref, lowpass_ref, recv_ref, out_ref, resampled_ref, weight_ref, product_ref = refs
    sources, rows, wide = recv_ref.shape
    dates = shift_ref.shape[0]
    az_count = sources // dates
    own_lines = rows // 2
    lines = own_lines * az_count
    groups = lines // LOOK_AZ
    looks = chunk // LOOK_RG
    table = table_ref[...]
    held = resampled_ref.shape[2]

    out_row = lax.broadcasted_iota(jnp.int32, (lines, lines), 0)
    in_row = lax.broadcasted_iota(jnp.int32, (lines, lines), 1)
    line = LOOK_AZ * (out_row % groups) + out_row // groups
    line_distance = (in_row - line + 3).astype(jnp.float32)
    span = min(2 * LANES, wide)
    column_distance = (
        lax.broadcasted_iota(jnp.int32, (span, LANES), 0) - lax.broadcasted_iota(jnp.int32, (span, LANES), 1)
    ).astype(jnp.float32)
    for date in range(dates):
        numbers = recv_ref[date * az_count, 0:16, wide - LANES :].astype(jnp.float32)[0:1, LANES - META :]
        line_offset, line_index, column_index = (numbers[:, s : s + 1] for s in range(META))
        line_taps = banded(picked_taps(table, line_index), line_distance - line_offset)
        line_taps = jnp.concatenate(halves(line_taps), axis=0)
        column_high, column_low = halves(banded(picked_taps(table, column_index), column_distance))
        moved = []
        for plane in range(2):
            rows_of = slice(plane * own_lines, (plane + 1) * own_lines)
            source = jnp.concatenate([recv_ref[date * az_count + a, rows_of, :] for a in range(az_count)], axis=0)
            both = dot(line_taps, source)
            moved.append(both[:lines] + both[lines:])
        moved_high, moved_low = halves(jnp.concatenate(moved, axis=0))
        for begin in range(0, held, LANES):
            end = min(begin + span, wide)
            taken = end - begin
            total = dot(moved_high[:, begin:end], column_high[:taken])
            total += dot(moved_low[:, begin:end], column_high[:taken])
            total += dot(moved_high[:, begin:end], column_low[:taken])
            resampled_ref[date, :, begin : begin + LANES] = total.astype(jnp.bfloat16)

    window = lowpass_ref[...]
    spacing = lax.broadcasted_iota(jnp.int32, window.shape, 1).astype(jnp.float32) - FILTER_HALF
    span = min(2 * LANES, held)

    def one_pair(place, own, other):
        gap = shift_ref[own] - shift_ref[other]
        angle = jnp.where(jnp.abs(spacing) <= FILTER_HALF, jnp.pi * gap * spacing, 0.0)
        for part, taps in enumerate((window * jnp.cos(angle), window * jnp.sin(angle))):
            spread = jnp.broadcast_to(taps, (LANES, 2 * LANES))
            spread = pltpu.roll(spread, 0, 1, stride=1, stride_axis=0)
            high, low = halves(spread)
            weight_ref[0, part * LANES : (part + 1) * LANES, :] = high
            weight_ref[1, part * LANES : (part + 1) * LANES, :] = low
        both = jnp.concatenate([resampled_ref[own], resampled_ref[other]], axis=0)
        for begin in range(0, up(chunk, LANES), LANES):
            end = min(begin + span, held)
            taken = end - begin
            total = dot_nt(both[:, begin:end], weight_ref[0, :, :taken])
            total += dot_nt(both[:, begin:end], weight_ref[1, :, :taken])
            cos, sin = total[:, :LANES], total[:, LANES:]
            re, im = slice(0, lines), slice(lines, 2 * lines)
            master_re = cos[re] + sin[im]
            master_im = cos[im] - sin[re]
            re, im = slice(2 * lines, 3 * lines), slice(3 * lines, 4 * lines)
            partner_re = cos[re] - sin[im]
            partner_im = cos[im] + sin[re]
            for part, product in enumerate(
                (
                    master_re * partner_re + master_im * partner_im,
                    master_im * partner_re - master_re * partner_im,
                )
            ):
                summed = sum(product[k * groups : (k + 1) * groups] for k in range(LOOK_AZ))
                product_ref[place, part, :, begin : begin + LANES] = summed

    if isinstance(pairs, int):
        count = pairs

        def step(place, carry):
            one_pair(place, table_of_pairs[place, 0], table_of_pairs[place, 1])
            return carry

        lax.fori_loop(0, count, step, 0)
    else:
        count = len(pairs)
        for place, (own, other) in enumerate(pairs):
            one_pair(place, own, other)

    out_width = out_ref.shape[2]
    column = lax.broadcasted_iota(jnp.int32, (product_ref.shape[3], out_width), 0)
    lane = lax.broadcasted_iota(jnp.int32, (product_ref.shape[3], out_width), 1)
    collect = jnp.where(column // LOOK_RG == lane % looks, 1.0, 0.0).astype(jnp.bfloat16)
    high, low = halves(product_ref[...].reshape(count * 2 * groups, product_ref.shape[3]))
    total = (dot(high, collect) + dot(low, collect)) * (1.0 / (LOOK_AZ * LOOK_RG))
    total = total.reshape(count, 2, groups, out_width)
    own_lane = lax.broadcasted_iota(jnp.int32, (groups, out_width), 1) // looks
    place = 0
    for own in range(dates):
        value = jnp.zeros((groups, out_width), jnp.float32)
        for lag in range(min(LAGS, dates - 1 - own)):
            for part in range(2):
                value = jnp.where(own_lane == lag * 2 + part, total[place, part], value)
            place += 1
        out_ref[own * az_count : (own + 1) * az_count] = value.reshape(az_count, groups // az_count, out_width)


def unpack_kernel(used_lags, looks, recv_ref, out_ref):
    sources, groups, width = recv_ref.shape
    columns = out_ref.shape[-1]
    lane = lax.broadcasted_iota(jnp.int32, (groups, columns), 1) // looks
    out_ref[...] = jnp.zeros_like(out_ref)
    for lag in range(used_lags):
        for part in range(2):
            value = jnp.zeros((groups, columns), jnp.float32)
            for source in range(sources):
                block = recv_ref[source]
                if width != columns:
                    block = block[:, :columns]
                shift = looks * (source - lag * 2 - part) % columns
                if shift:
                    block = pltpu.roll(block, shift, 1)
                value = jnp.where(lane == source, block, value)
            out_ref[part, lag] = value


def chunked_body(slc, offsets, kernel_index, range_shift):
    axes = ("date", "az")
    date_count, az_count, rng_count = (lax.axis_size(a) for a in ("date", "az", "rng"))
    peers = date_count * az_count
    lines, columns = slc.shape[2], slc.shape[3]
    dates = range_shift.shape[0]
    chunk = columns // peers
    looks = chunk // LOOK_RG
    groups = lines * az_count // LOOK_AZ
    wide = up(chunk + 2 * FILTER_HALF + TAPS - 1 + META, LANES)
    held = up(chunk + 2 * FILTER_HALF, LANES)
    used_lags = min(LAGS, dates - 1)
    out_width = up(used_lags * 2 * looks, LANES)
    vmem = pl.BlockSpec(memory_space=pltpu.VMEM)
    smem = pl.BlockSpec(memory_space=pltpu.SMEM)
    limit = pltpu.CompilerParams(vmem_limit_bytes=32 * 1024 * 1024)

    cells = slc.reshape(2 * lines, columns)
    place = lax.axis_index("rng")
    if rng_count == 2:
        edge = jnp.where(place == 0, cells[:, columns - LANES :], cells[:, :LANES])
        before = after = lax.ppermute(edge, "rng", [(0, 1), (1, 0)])
    else:
        forth = [(i, i + 1) for i in range(rng_count - 1)]
        before = lax.ppermute(cells[:, columns - LANES :], "rng", forth)
        after = lax.ppermute(cells[:, :LANES], "rng", [(b, a) for a, b in forth])

    packed = pl.pallas_call(
        functools.partial(pack_kernel, chunk),
        out_shape=jax.ShapeDtypeStruct((peers, 2 * lines, wide), jnp.bfloat16),
        in_specs=[smem] * 3 + [vmem] * 3,
        out_specs=vmem,
        scratch_shapes=[pltpu.VMEM((2 * lines, columns + 2 * LANES), jnp.bfloat16)],
        compiler_params=limit,
    )(jnp.stack([place, rng_count]).astype(jnp.int32), offsets, kernel_index, cells, before, after)
    arrived = lax.all_to_all(packed, axes, 0, 0, tiled=True)

    pairs = [(own, own + lag) for own in range(dates) for lag in range(1, LAGS + 1) if own + lag < dates]
    count = len(pairs)
    first = [jnp.asarray(np.array(pairs, np.int32))] if count > UNROLLED_PAIRS else []
    looked = pl.pallas_call(
        functools.partial(pairs_kernel, chunk, count if first else pairs),
        out_shape=jax.ShapeDtypeStruct((peers, groups // az_count, out_width), jnp.float32),
        in_specs=[smem] * len(first) + [smem] + [vmem] * 3,
        out_specs=vmem,
        scratch_shapes=[
            pltpu.VMEM((dates, 4 * (groups * LOOK_AZ) // 2, held), jnp.bfloat16),
            pltpu.VMEM((2, 2 * LANES, 2 * LANES), jnp.bfloat16),
            pltpu.VMEM((count, 2, groups, up(chunk, LANES)), jnp.float32),
        ],
        compiler_params=limit,
    )(*first, range_shift, jnp.asarray(kernel_table()), jnp.asarray(lowpass_row(2 * LANES)), arrived)
    returned = lax.all_to_all(looked, axes, 0, 0, tiled=True)

    out = pl.pallas_call(
        functools.partial(unpack_kernel, used_lags, looks),
        out_shape=jax.ShapeDtypeStruct((2, LAGS, groups // az_count, looks * peers), jnp.float32),
        in_specs=[vmem],
        out_specs=vmem,
        compiler_params=limit,
    )(returned)
    return out[:, None]


HALO_LINES = 16
FOLD = 16
TAIL = 2 * FILTER_HALF


def sinc(value):
    angle = jnp.pi * value
    return jnp.where(angle == 0.0, 1.0, jnp.sin(angle) / jnp.where(angle == 0.0, 1.0, angle))


def tap_row(index):
    lane = lax.broadcasted_iota(jnp.int32, (1, LANES), 1)
    position = lane.astype(jnp.float32) - 3.0 - index.astype(jnp.float32) / KERNELS
    shaped = sinc(position) * (0.5 + 0.5 * jnp.cos(jnp.pi * position / 5.0))
    shaped = jnp.where(lane < TAPS, shaped, 0.0)
    return shaped / jnp.sum(shaped, axis=1, keepdims=True)


def row_line(row, az):
    quarter = HALO_LINES // LOOK_AZ
    within = row % HALO_LINES
    return HALO_LINES * ((row // HALO_LINES) ^ az) + LOOK_AZ * (within % quarter) + within // quarter


def prepare_kernel(offsets_hbm, index_hbm, slc_ref, side_ref, corner_ref, lines_ref, line_ref, column_ref, held_ref, offsets_ref, index_ref, semaphores):
    lines, columns = slc_ref.shape[1:]
    az = lax.axis_index("az")
    row = pl.multiple_of((1 - az) * (lines - HALO_LINES), HALO_LINES)
    edge = pl.multiple_of((1 - lax.axis_index("rng")) * (columns - LANES), LANES)
    nearest, outermost = pl.ds(row, HALO_LINES), pl.ds(edge, LANES)
    moves = [
        (offsets_hbm, offsets_ref),
        (index_hbm, index_ref),
        (slc_ref.at[:, :, outermost], side_ref),
        (slc_ref.at[:, nearest, outermost], corner_ref),
        (slc_ref.at[:, nearest, :], lines_ref),
        (slc_ref, held_ref.at[:, :, pl.ds(LANES, columns)]),
    ]
    copies = [pltpu.make_async_copy(a, b, semaphores.at[i]) for i, (a, b) in enumerate(moves)]
    for copy in copies:
        copy.start()
    held_ref[:, :, :LANES] = jnp.zeros((2, lines, LANES), held_ref.dtype)
    held_ref[:, :, LANES + columns :] = jnp.zeros((2, lines, 2 * LANES), held_ref.dtype)
    copies[0].wait()
    copies[1].wait()
    for half in range(2):
        shape = (HALO_LINES, lines + HALO_LINES)
        line = row_line(lax.broadcasted_iota(jnp.int32, shape, 0) + half * HALO_LINES, az)
        place = lax.broadcasted_iota(jnp.int32, shape, 1)
        source = jnp.where(place < lines, place, place + jnp.where(az == 0, 0, -lines - HALO_LINES))
        taps = banded(tap_row(index_ref[0, 0]), source - line - offsets_ref[0, 0] + 3)
        line_ref[half] = jnp.concatenate(halves(taps), axis=0)
    shape = (3 * LANES, LANES)
    distance = lax.broadcasted_iota(jnp.int32, shape, 0) - lax.broadcasted_iota(jnp.int32, shape, 1)
    distance = distance - (LANES - FILTER_HALF - 3) - offsets_ref[0, 1]
    taps = banded(tap_row(index_ref[0, 1]), distance)
    column_ref[...] = jnp.concatenate(halves(taps), axis=1)
    for copy in copies[2:]:
        copy.wait()


def along_range(moved, column_ref, tiles):
    high, low = halves(moved)
    starts = range(0, tiles * LANES, LANES)
    high = jnp.concatenate([high[:, s : s + 3 * LANES] for s in starts], axis=0)
    low = jnp.concatenate([low[:, s : s + 3 * LANES] for s in starts], axis=0)
    total = dot(high, column_ref[...])
    return total[:, :LANES] + total[:, LANES:] + dot(low, column_ref[:, :LANES])


def early_kernel(tiles, held_ref, line_ref, column_ref, out_ref):
    lines = held_ref.shape[1]
    early = out_ref.shape[0] // (2 * HALO_LINES)
    chunk = lax.axis_index("date") ^ (lax.axis_size("date") - 1)
    begin = pl.multiple_of((chunk * tiles + lax.axis_index("rng")) * LANES, LANES)
    moved = []
    for plane in range(2):
        both = dot(line_ref[0, :, :lines], held_ref[plane, :, pl.ds(begin, (early + 2) * LANES)])
        moved.append(both[:HALO_LINES] + both[HALO_LINES:])
    moved = jnp.concatenate(moved, axis=0)
    out_ref[...] = along_range(moved, column_ref, early).astype(jnp.bfloat16)


def whole_lines(taps, sources):
    moved = [[], []]
    for source in sources:
        both = dot(taps, source)
        for half in range(2):
            at = 2 * half * HALO_LINES
            moved[half].append(both[at : at + HALO_LINES] + both[at + HALO_LINES : at + 2 * HALO_LINES])
    return jnp.concatenate(moved[0] + moved[1], axis=0)


def folded_tail(tile):
    lane = lax.broadcasted_iota(jnp.int32, (FOLD, LANES), 1) // TAIL
    folded = tile[:FOLD]
    for part in range(1, tile.shape[0] // FOLD):
        folded = jnp.where(lane == part, pltpu.roll(tile[part * FOLD : (part + 1) * FOLD], part * TAIL, 1), folded)
    return folded.astype(jnp.bfloat16)


def first_kernel(tiles, step, side_ref, corner_ref, lines_ref, held_ref, line_ref, column_ref, out_ref, wide_ref):
    lines, width = held_ref.shape[1:]
    block = lax.axis_index("rng")
    zero = jnp.zeros((lines, LANES), wide_ref.dtype)
    for plane in range(2):
        side, corner = side_ref[plane], corner_ref[plane]
        right = width - 2 * LANES
        wide_ref[plane, :lines, :LANES] = jnp.where(block > 0, side, zero)
        wide_ref[plane, :lines, LANES:right] = held_ref[plane, :, LANES:right]
        wide_ref[plane, :lines, right : right + LANES] = jnp.where(block == 0, side, zero)
        wide_ref[plane, :lines, right + LANES :] = zero
        wide_ref[plane, lines:, :LANES] = jnp.where(block > 0, corner, zero[:HALO_LINES])
        wide_ref[plane, lines:, LANES:right] = lines_ref[plane]
        wide_ref[plane, lines:, right : right + LANES] = jnp.where(block == 0, corner, zero[:HALO_LINES])
        wide_ref[plane, lines:, right + LANES :] = zero[:HALO_LINES]
    taps = jnp.concatenate([line_ref[0], line_ref[1]], axis=0)
    chunk = lax.axis_index("date") ^ step
    read = pl.ds(pl.multiple_of(chunk * tiles * LANES, LANES), (tiles + 3) * LANES)
    moved = whole_lines(taps, [wide_ref[plane, :, read] for plane in range(2)])
    total = along_range(moved, column_ref, tiles + 1)
    rows = tiles * 2 * lines
    out_ref[:rows] = total[:rows].astype(jnp.bfloat16)
    out_ref[rows : rows + FOLD] = folded_tail(total[rows:])
    out_ref[rows + FOLD :] = jnp.zeros((out_ref.shape[0] - rows - FOLD, LANES), out_ref.dtype)


def rest_kernel(tiles, steps, wide_ref, line_ref, column_ref, *outs):
    lines = wide_ref.shape[1] - HALO_LINES
    block = lax.axis_index("rng")
    date = lax.axis_index("date")
    taps = jnp.concatenate([line_ref[0], line_ref[1]], axis=0)
    rows = 2 * lines
    for step, out_ref in zip(steps, outs):
        read = pl.ds(pl.multiple_of((date ^ step) * tiles * LANES, LANES), (tiles + 3) * LANES)
        moved = whole_lines(taps, [wide_ref[plane, :, read] for plane in range(2)])
        total = along_range(moved, column_ref, tiles + 1)
        tail = folded_tail(total[tiles * rows :])
        total = total.astype(jnp.bfloat16)
        if out_ref.shape[0] == tiles * rows + FOLD:
            out_ref[: tiles * rows] = total[: tiles * rows]
            out_ref[tiles * rows :] = tail
            continue
        for tile in range(tiles - 1):
            near, far = (total[at * rows + lines : (at + 1) * rows] for at in (tile, tile + 1))
            out_ref[tile * lines : (tile + 1) * lines] = jnp.where(block == 0, near, far)
        begin = (tiles - 1) * rows
        out_ref[begin // 2 : begin // 2 + rows] = jnp.where(block == 0, total[begin : begin + rows], total[:rows])
        out_ref[begin // 2 + rows :] = tail


def filter_kernel(pairs, shift_hbm, early_ref, out_ref, spread_ref, shift_ref, semaphore):
    copy = pltpu.make_async_copy(shift_hbm, shift_ref, semaphore)
    copy.start()
    lines = 2 * HALO_LINES
    spread_ref[...] = jnp.zeros_like(spread_ref)
    for tile in range(early_ref.shape[0] // lines):
        begin = pl.multiple_of((tile + lax.axis_index("rng")) * 2 * lines, FOLD)
        spread_ref[pl.ds(begin, lines), :] = early_ref[tile * lines : (tile + 1) * lines]
    date = lax.axis_index("date")
    spacing = lax.broadcasted_iota(jnp.int32, (1, 2 * LANES), 1).astype(jnp.float32) - FILTER_HALF
    window = 0.4 * sinc(0.4 * spacing) * (0.54 + 0.46 * jnp.cos(jnp.pi * spacing / (FILTER_HALF + 1)))
    window = jnp.where(jnp.abs(spacing) <= FILTER_HALF, window, 0.0)
    copy.wait()
    for place, (first, second) in enumerate(pairs):
        gap = shift_ref[date ^ first] - shift_ref[date ^ second]
        angle = jnp.where(jnp.abs(spacing) <= FILTER_HALF, jnp.pi * gap * spacing, 0.0)
        for part, taps in enumerate((window * jnp.cos(angle), window * jnp.sin(angle))):
            spread = jnp.broadcast_to(taps, (LANES, 2 * LANES))
            spread = pltpu.roll(spread, 0, 1, stride=1, stride_axis=0)
            high, low = halves(spread)
            out_ref[place, 0, part * LANES : (part + 1) * LANES, :] = high
            out_ref[place, 1, part * LANES : (part + 1) * LANES, :] = low


def looks_kernel(pairs, dates, weight_ref, *refs):
    early_ref, chunks, outs = refs[0], list(refs[1 : dates + 1][::-1]), refs[dates + 1 : 2 * dates + 1]
    whole_ref, window_ref, product_ref = refs[-3:]
    groups, lines = outs[0].shape[0], outs[0].shape[0] * LOOK_AZ
    rows = 2 * lines
    blocks = (chunks[0].shape[0] - FOLD) // rows
    looks = blocks * LANES // LOOK_RG
    date = lax.axis_index("date")
    block = lax.axis_index("rng")
    early = blocks - 1
    whole_ref[: blocks * rows] = early_ref[...]
    for tile in range(early):
        begin = pl.multiple_of((tile + block) * rows, FOLD)
        whole_ref[pl.ds(begin + lines, lines), :] = chunks[-1][tile * lines : (tile + 1) * lines]
    begin = pl.multiple_of((1 - block) * early * rows, FOLD)
    whole_ref[pl.ds(begin, rows), :] = chunks[-1][early * lines : early * lines + rows]
    whole_ref[blocks * rows :] = chunks[-1][early * lines + rows :]
    chunks[-1] = whole_ref
    az = lax.axis_index("az")
    upper = lax.broadcasted_iota(jnp.int32, (groups, LANES), 0) // (groups // 2) == az
    for step, chunk_ref in enumerate(chunks):
        window_ref[step, :, :LANES] = chunk_ref[: blocks * rows]
        window_ref[step, : (blocks - 1) * rows, LANES:] = chunk_ref[rows : blocks * rows]
        folded = chunk_ref[blocks * rows : blocks * rows + FOLD].astype(jnp.float32)
        for part in range(rows // FOLD):
            value = pltpu.roll(folded, LANES - part * TAIL, 1) if part else folded
            at = pl.ds((blocks - 1) * rows + part * FOLD, FOLD)
            window_ref[step, at, LANES:] = value.astype(jnp.bfloat16)
    for place, (first, second) in enumerate(pairs):
        def filtered(step):
            total = dot_nt(window_ref[step], weight_ref[place, 0]) + dot_nt(window_ref[step], weight_ref[place, 1])
            total = total.reshape(blocks, 2, 2, HALO_LINES, 2 * LANES)
            re, im = total[:, :, 0], total[:, :, 1]
            return re[..., :LANES], im[..., :LANES], re[..., LANES:], im[..., LANES:]

        cos_re, cos_im, sin_re, sin_im = filtered(first)
        master_re, master_im = cos_re + sin_im, cos_im - sin_re
        cos_re, cos_im, sin_re, sin_im = filtered(second)
        partner_re, partner_im = cos_re - sin_im, cos_im + sin_re
        for part, product in enumerate(
            (
                master_re * partner_re + master_im * partner_im,
                master_im * partner_re - master_re * partner_im,
            )
        ):
            summed = product[:, :, :groups] + product[:, :, groups:]
            at = pl.ds((place * 2 + part) * groups, groups)
            for k in range(blocks):
                both = [summed[k, half] + pltpu.roll(summed[k, half], groups // 2, 0) for half in range(2)]
                product_ref[at, k * LANES : (k + 1) * LANES] = jnp.where(upper, both[0], both[1])

    out_width = outs[0].shape[1]
    column = lax.broadcasted_iota(jnp.int32, (product_ref.shape[1], out_width), 0)
    lane = lax.broadcasted_iota(jnp.int32, (product_ref.shape[1], out_width), 1)
    collect = jnp.where(column // LOOK_RG == lane % looks, 1.0, 0.0).astype(jnp.bfloat16)
    high, low = halves(product_ref[...])
    total = (dot(high, collect) + dot(low, collect)) * (1.0 / (LOOK_AZ * LOOK_RG))
    total = total.reshape(len(pairs), 2, groups, out_width)
    own_lane = lax.broadcasted_iota(jnp.int32, (groups, out_width), 1) // looks
    for step, out_ref in enumerate(outs):
        value = jnp.zeros((groups, out_width), jnp.float32)
        for place, pair in enumerate(pairs):
            if step in pair:
                other = pair[1] if pair[0] == step else pair[0]
                lag = (date ^ other) - (date ^ step)
                for part in range(2):
                    signed = -total[place, part] if part == 1 and pair[1] == step else total[place, part]
                    value = jnp.where(own_lane == (lag - 1) * 2 + part, signed, value)
        out_ref[...] = value


def place_kernel(used_lags, looks, *refs):
    out_ref = refs[-1]
    groups, columns = out_ref.shape[2:]
    date = lax.axis_index("date")
    lane = lax.broadcasted_iota(jnp.int32, (groups, LANES), 1) // looks
    out_ref[...] = jnp.zeros_like(out_ref)
    each = LANES // looks
    for step, recv_ref in enumerate(refs[:-1][::-1]):
        chunk = date ^ step
        for lag in range(used_lags):
            for part in range(2):
                tile, group = divmod(lag * 2 + part, each)
                block = recv_ref[:, tile * LANES : (tile + 1) * LANES]
                block = pltpu.roll(block, lax.bitwise_and(looks * (chunk - group), LANES - 1), 1)
                out_ref[part, lag] = jnp.where(lane == chunk, block, out_ref[part, lag])


def tiled_body(slc, offsets, kernel_index, range_shift):
    dates = lax.axis_size("date")
    lines, columns = slc.shape[2], slc.shape[3]
    chunk = columns // dates
    looks = chunk // LOOK_RG
    groups = lines // LOOK_AZ
    out_width = up(min(LAGS, dates - 1) * 2 * looks, LANES)
    vmem = pl.BlockSpec(memory_space=pltpu.VMEM)
    hbm = pl.BlockSpec(memory_space=pltpu.HBM)
    limit = pltpu.CompilerParams(vmem_limit_bytes=32 * 1024 * 1024)
    bf16 = jnp.bfloat16
    cells, offsets, kernel_index, range_shift = (
        pltpu.with_memory_space_constraint(value, pltpu.HBM)
        for value in (slc.reshape(2, lines, columns), offsets, kernel_index, range_shift)
    )
    tiles = chunk // LANES
    chunk_rows = tiles * 2 * lines

    side, corner, halo_lines, line_taps, column_taps, held = pl.pallas_call(
        prepare_kernel,
        out_shape=[
            jax.ShapeDtypeStruct((2, lines, LANES), bf16),
            jax.ShapeDtypeStruct((2, HALO_LINES, LANES), bf16),
            jax.ShapeDtypeStruct((2, HALO_LINES, columns), bf16),
            jax.ShapeDtypeStruct((2, 2 * HALO_LINES, lines + HALO_LINES), bf16),
            jax.ShapeDtypeStruct((3 * LANES, 2 * LANES), bf16),
            jax.ShapeDtypeStruct((2, lines, columns + 3 * LANES), bf16),
        ],
        in_specs=[hbm] * 3,
        out_specs=[vmem] * 6,
        scratch_shapes=[
            pltpu.SMEM(offsets.shape, jnp.int32),
            pltpu.SMEM(kernel_index.shape, jnp.int32),
            pltpu.SemaphoreType.DMA((6,)),
        ],
        compiler_params=limit,
    )(offsets, kernel_index, cells)
    swap = [(0, 1), (1, 0)]
    side = lax.ppermute(side, "rng", swap)
    corner = lax.ppermute(corner, ("rng", "az"), [(0, 3), (1, 2), (2, 1), (3, 0)])
    halo_lines = lax.ppermute(halo_lines, "az", swap)

    def swapped(value, step):
        return lax.ppermute(value, "date", [(i, i ^ step) for i in range(dates)])

    steps = range(dates - 1, 0, -1)
    early_rows = (tiles - 1) * lines
    early = pl.pallas_call(
        functools.partial(early_kernel, tiles),
        out_shape=jax.ShapeDtypeStruct((early_rows, LANES), bf16),
        in_specs=[vmem] * 3,
        out_specs=vmem,
        compiler_params=limit,
    )(held, line_taps, column_taps)
    early = swapped(early, steps[0])
    first, wide = pl.pallas_call(
        functools.partial(first_kernel, tiles, steps[1]),
        out_shape=[
            jax.ShapeDtypeStruct((chunk_rows + 2 * FOLD, LANES), bf16),
            jax.ShapeDtypeStruct((2, lines + HALO_LINES, columns + 3 * LANES), bf16),
        ],
        in_specs=[vmem] * 6,
        out_specs=[vmem] * 2,
        compiler_params=limit,
    )(side, corner, halo_lines, held, line_taps, column_taps)
    first = swapped(first, steps[1])
    others = [steps[0], *steps[2:], 0]
    rest = pl.pallas_call(
        functools.partial(rest_kernel, tiles, others),
        out_shape=[
            jax.ShapeDtypeStruct((chunk_rows + FOLD - (early_rows if step == steps[0] else 0), LANES), bf16)
            for step in others
        ],
        in_specs=[vmem] * 3,
        out_specs=[vmem] * (dates - 1),
        compiler_params=limit,
        cost_estimate=pl.CostEstimate(flops=400_000_000, bytes_accessed=0, transcendentals=0),
    )(wide, line_taps, column_taps)
    rest = [swapped(rows, step) if step else rows for rows, step in zip(rest, others)]
    chunks = [rest[0], first, *rest[1:]]

    pairs = [(first, second) for first in range(dates) for second in range(first + 1, dates)]
    weights, early = pl.pallas_call(
        functools.partial(filter_kernel, pairs),
        out_shape=[
            jax.ShapeDtypeStruct((len(pairs), 2, 2 * LANES, 2 * LANES), bf16),
            jax.ShapeDtypeStruct((chunk_rows, LANES), bf16),
        ],
        in_specs=[hbm, vmem],
        out_specs=[vmem] * 2,
        scratch_shapes=[pltpu.SMEM(range_shift.shape, jnp.float32), pltpu.SemaphoreType.DMA],
        compiler_params=limit,
        cost_estimate=pl.CostEstimate(flops=935_000_000, bytes_accessed=0, transcendentals=0),
    )(range_shift, early)
    looked = pl.pallas_call(
        functools.partial(looks_kernel, pairs, dates),
        out_shape=[jax.ShapeDtypeStruct((groups, out_width), jnp.float32)] * dates,
        in_specs=[vmem] * (2 + dates),
        out_specs=[vmem] * dates,
        scratch_shapes=[
            pltpu.VMEM((chunk_rows + FOLD, LANES), bf16),
            pltpu.VMEM((dates, chunk_rows, 2 * LANES), bf16),
            pltpu.VMEM((len(pairs) * 2 * groups, chunk), jnp.float32),
        ],
        compiler_params=limit,
    )(weights, early, *chunks)
    out = pl.pallas_call(
        functools.partial(place_kernel, min(LAGS, dates - 1), looks),
        out_shape=jax.ShapeDtypeStruct((2, LAGS, groups, looks * dates), jnp.float32),
        in_specs=[vmem] * dates,
        out_specs=vmem,
        compiler_params=limit,
    )(*[swapped(looked[step], step) for step in steps], looked[0])
    return out[:, None]


def body(slc, offsets, kernel_index, range_shift):
    dates, az_count = (lax.axis_size(a) for a in ("date", "az"))
    lines, columns = slc.shape[2], slc.shape[3]
    whole_tiles = columns % (dates * LANES) == 0 and columns % (dates * LOOK_RG) == 0
    one_row = columns // LOOK_RG == LANES and range_shift.shape[0] == dates
    few = dates & (dates - 1) == 0 and dates - 1 <= LAGS
    folds = lines == 2 * HALO_LINES and lax.axis_size("rng") == 2 and dates >= 4 and 2 * lines // FOLD * TAIL <= LANES
    if az_count == 2 and whole_tiles and one_row and few and folds:
        return tiled_body(slc, offsets, kernel_index, range_shift)
    return chunked_body(slc, offsets, kernel_index, range_shift)


def solution(mesh):
    return jax.shard_map(
        body,
        mesh=mesh,
        in_specs=(
            P(None, ("groups", "date"), "az", "rng"),
            P(("groups", "date"), None),
            P(("groups", "date"), None),
            P("groups"),
        ),
        out_specs=P(None, ("groups", "date"), None, "az", "rng"),
        check_vma=False,
    )
```

profile of v0, /device:TPU:0, one launch (start us, length us, event | category | flops | bytes accessed | tf_op | source)
XLA Modules:
  0.0 28.9 jit_solution(7873531177951796051)
XLA Ops:
  0.0 1.2 %shard_map.46 = (bf16[2,32,128]{2,1,0:T(8,128)(2,1)S(1)}, bf16[2,16,128]{2,1,0:T(8,128)(2,1)S(1)}, bf16[2,16,2560]{2,1,0:T(8,128)(2,1)S(1)}, bf16[2,32,48]{2,1,0...) custom-call(s32[1,2]{1,0:T(1,128)} %offsets_hbm.1, s32[1,2]{1,0:T(1,128)} %index_hbm.1, ...), custom_call_target="tpu_custom_call" | custom-call | tf_op jit(solution)/shard_map/pallas_call | solution.py:562
  1.2 0.5 %collective-permute-start.3 = (bf16[2,16,2560]{2,1,0:T(8,128)(2,1)S(1)}, bf16[2,16,2560]{2,1,0:T(8,128)(2,1)S(1)}, u32[]{:S(2)}, u32[]{:S(2)}) collective-permute-start(bf16[2,16,2560]{2,1,0:T(8,128)(2,1)S(1)} %get-tuple-element.29), channel_id=1, source_target_pairs={{0,1},{1,0},{2,3},{3,2},{4,5},{5,4},{6,7},{7,6},{8,9},{9,8},{10,11... | collective-permute-start | bytes 491528 | tf_op jit(solution)/shard_map/ppermute | solution.py:584
  1.7 2.6 %collective-permute-start.1 = (bf16[2,32,128]{2,1,0:T(8,128)(2,1)S(1)}, bf16[2,32,128]{2,1,0:T(8,128)(2,1)S(1)}, u32[]{:S(2)}, u32[]{:S(2)}) collective-permute-start(bf16[2,32,128]{2,1,0:T(8,128)(2,1)S(1)} %get-tuple-element.27), channel_id=1, source_target_pairs={{0,2},{2,0},{1,3},{3,1},{4,6},{6,4},{5,7},{7,5},{8,10},{10,8},{9,1... | collective-permute-start | bytes 49160 | tf_op jit(solution)/shard_map/ppermute | solution.py:582
  4.3 0.1 collective-permute-start.2
  4.4 0.3 %shard_map.47 = bf16[128,128]{1,0:T(8,128)(2,1)S(1)} custom-call(bf16[2,32,2944]{2,1,0:T(8,128)(2,1)S(1)} %get-tuple-element.22.held_ref, bf16[2,32,48]{2,1,0:T(8,128)(2,1)S(1)} %get-tuple-element.23.line_ref, bf16[384,256]{1,0:T(8,128)(2,1)S(1)} %get-tuple-element.24.column_ref), custom_call_target="tpu_custom_call" | custom-call | tf_op jit(solution)/shard_map/pallas_call | solution.py:591
  4.7 3.9 %collective-permute-start = (bf16[128,128]{1,0:T(8,128)(2,1)S(1)}, bf16[128,128]{1,0:T(8,128)(2,1)S(1)}, u32[]{:S(2)}, u32[]{:S(2)}) collective-permute-start(bf16[128,128]{1,0:T(8,128)(2,1)S(1)} %shard_map.47), channel_id=1, source_target_pairs={{0,12},{4,8},{8,4},{12,0},{1,13},{5,9},{9,5},{13,1},{2,14},{6,10},... | collective-permute-start | bytes 98312 | tf_op jit(solution)/shard_map/ppermute | solution.py:587
  8.6 0.0 collective-permute-done.2.corner_ref
  8.6 0.0 collective-permute-done.1.side_ref
  8.6 0.0 collective-permute-done.3.lines_ref
  8.6 0.6 %shard_map.49 = (bf16[352,128]{1,0:T(8,128)(2,1)S(1)}, bf16[2,48,2944]{2,1,0:T(8,128)(2,1)S(1)}) custom-call(bf16[2,32,128]{2,1,0:T(8,128)(2,1)S(1)} %collective-permute-done.1.side_ref, bf16[2,16,128]{2,1,0:T(8,128)(2,1)S(1)} %collective-permute-done.2.corner_ref, bf16[2,16,2560]{2,1,0:T(8,128)(2,1)S(1)} %collective-permute-done.3.lines_ref, ...), custom_call_target="tpu_custom_call" | custom-call | tf_op jit(solution)/shard_map/pallas_call | solution.py:599
  9.3 1.3 %collective-permute-start.5 = (bf16[352,128]{1,0:T(8,128)(2,1)S(1)}, bf16[352,128]{1,0:T(8,128)(2,1)S(1)}, u32[]{:S(2)}, u32[]{:S(2)}) collective-permute-start(bf16[352,128]{1,0:T(8,128)(2,1)S(1)} %get-tuple-element.32), channel_id=1, source_target_pairs={{0,8},{4,12},{8,0},{12,4},{1,9},{5,13},{9,1},{13,5},{2,10},{6,14},... | collective-permute-start | bytes 270344 | tf_op jit(solution)/shard_map/ppermute | solution.py:587
  10.6 1.4 %shard_map.50 = (bf16[208,128]{1,0:T(8,128)(2,1)S(1)}, bf16[336,128]{1,0:T(8,128)(2,1)S(1)}, bf16[336,128]{1,0:T(8,128)(2,1)S(1)}) custom-call(bf16[2,48,2944]{2,1,0:T(8,128)(2,1)S(1)} %get-tuple-element.30.wide_ref, bf16[2,32,48]{2,1,0:T(8,128)(2,1)S(1)} %get-tuple-element.23.line_ref, bf16[384,256]{1,0:T(8,128)(2,1)S(1)} %get-tuple-element.24.column_ref), custom_call_target="tpu_custom_call" | custom-call | flops 400000000 | tf_op jit(solution)/shard_map/pallas_call | solution.py:611
  12.0 1.4 %collective-permute-start.4 = (bf16[208,128]{1,0:T(8,128)(2,1)S(1)}, bf16[208,128]{1,0:T(8,128)(2,1)S(1)}, u32[]{:S(2)}, u32[]{:S(2)}) collective-permute-start(bf16[208,128]{1,0:T(8,128)(2,1)S(1)} %get-tuple-element.31), channel_id=1, source_target_pairs={{0,12},{4,8},{8,4},{12,0},{1,13},{5,9},{9,5},{13,1},{2,14},{6,10},... | collective-permute-start | bytes 159752 | tf_op jit(solution)/shard_map/ppermute | solution.py:587
  13.3 0.8 %collective-permute-start.6 = (bf16[336,128]{1,0:T(8,128)(2,1)S(1)}, bf16[336,128]{1,0:T(8,128)(2,1)S(1)}, u32[]{:S(2)}, u32[]{:S(2)}) collective-permute-start(bf16[336,128]{1,0:T(8,128)(2,1)S(1)} %get-tuple-element.33), channel_id=1, source_target_pairs={{0,4},{4,0},{8,12},{12,8},{1,5},{5,1},{9,13},{13,9},{2,6},{6,2},{1... | collective-permute-start | bytes 258056 | tf_op jit(solution)/shard_map/ppermute | solution.py:587
  14.1 0.0 collective-permute-done.early_ref
  14.1 1.2 %shard_map.48 = (bf16[6,2,256,256]{3,2,1,0:T(8,128)(2,1)S(1)}, bf16[320,128]{1,0:T(8,128)(2,1)S(1)}) custom-call(f32[4]{0:T(128)} %shift_hbm.1, bf16[128,128]{1,0:T(8,128)(2,1)S(1)} %collective-permute-done.early_ref), custom_call_target="tpu_custom_call" | custom-call | flops 935000000 | tf_op jit(solution)/shard_map/pallas_call | solution.py:626
  15.4 3.0 %collective-permute-done.4.refs_1_ = bf16[208,128]{1,0:T(8,128)(2,1)S(1)} collective-permute-done((bf16[208,128]{1,0:T(8,128)(2,1)S(1)}, bf16[208,128]{1,0:T(8,128)(2,1)S(1)}, u32[]{:S(2)}, u32[]{:S(2)}) %collective-permute-start.4) | collective-permute-done | bytes 53280 | tf_op jit(solution)/shard_map/ppermute | solution.py:587
  18.3 1.2 %collective-permute-done.6.refs_3_ = bf16[336,128]{1,0:T(8,128)(2,1)S(1)} collective-permute-done((bf16[336,128]{1,0:T(8,128)(2,1)S(1)}, bf16[336,128]{1,0:T(8,128)(2,1)S(1)}, u32[]{:S(2)}, u32[]{:S(2)}) %collective-permute-start.6) | collective-permute-done | bytes 86048 | tf_op jit(solution)/shard_map/ppermute | solution.py:587
  19.5 0.0 collective-permute-done.5.refs_2_
  19.5 1.6 %shard_map.51 = (f32[8,256]{1,0:T(8,128)S(1)}, f32[8,256]{1,0:T(8,128)S(1)}, f32[8,256]{1,0:T(8,128)S(1)}, f32[8,256]{1,0:T(8,128)S(1)}) custom-call(bf16[6,2,256,256]{3,2,1,0:T(8,128)(2,1)S(1)} %get-tuple-element.25.weight_ref, bf16[320,128]{1,0:T(8,128)(2,1)S(1)} %get-tuple-element.26.refs_0_, bf16[208,128]{1,0:T(8,128)(2,1)S(1)} %collective-permute-done.4.refs_1_, ...), custom_call_target="tpu_custom_call" | custom-call | tf_op jit(solution)/shard_map/pallas_call | solution.py:638
  21.1 2.5 %collective-permute-start.7 = (f32[8,256]{1,0:T(8,128)S(1)}, f32[8,256]{1,0:T(8,128)S(1)}, u32[]{:S(2)}, u32[]{:S(2)}) collective-permute-start(f32[8,256]{1,0:T(8,128)S(1)} %get-tuple-element.35), channel_id=1, source_target_pairs={{0,12},{4,8},{8,4},{12,0},{1,13},{5,9},{9,5},{13,1},{2,14},{6,10},... | collective-permute-start | bytes 24584 | tf_op jit(solution)/shard_map/ppermute | solution.py:587
  23.7 0.0 collective-permute-start.8
  23.7 1.9 %collective-permute-start.9 = (f32[8,256]{1,0:T(8,128)S(1)}, f32[8,256]{1,0:T(8,128)S(1)}, u32[]{:S(2)}, u32[]{:S(2)}) collective-permute-start(f32[8,256]{1,0:T(8,128)S(1)} %get-tuple-element.37), channel_id=1, source_target_pairs={{0,4},{4,0},{8,12},{12,8},{1,5},{5,1},{9,13},{13,9},{2,6},{6,2},{1... | collective-permute-start | bytes 24584 | tf_op jit(solution)/shard_map/ppermute | solution.py:587
  25.6 1.1 %collective-permute-done.7.refs_0_ = f32[8,256]{1,0:T(8,128)S(1)} collective-permute-done((f32[8,256]{1,0:T(8,128)S(1)}, f32[8,256]{1,0:T(8,128)S(1)}, u32[]{:S(2)}, u32[]{:S(2)}) %collective-permute-start.7) | collective-permute-done | bytes 8224 | tf_op jit(solution)/shard_map/ppermute | solution.py:587
  26.6 1.6 %collective-permute-done.8.refs_1_ = f32[8,256]{1,0:T(8,128)S(1)} collective-permute-done((f32[8,256]{1,0:T(8,128)S(1)}, f32[8,256]{1,0:T(8,128)S(1)}, u32[]{:S(2)}, u32[]{:S(2)}) %collective-permute-start.8) | collective-permute-done | bytes 8224 | tf_op jit(solution)/shard_map/ppermute | solution.py:587
  28.2 0.0 collective-permute-done.9.refs_2_
  28.2 0.7 %shard_map.52 = f32[2,8,8,128]{3,2,1,0:T(8,128)} custom-call(f32[8,256]{1,0:T(8,128)S(1)} %collective-permute-done.7.refs_0_, f32[8,256]{1,0:T(8,128)S(1)} %collective-permute-done.8.refs_1_, f32[8,256]{1,0:T(8,128)S(1)} %collective-permute-done.9.refs_2_, f32[8,256]{1,0:T(8,128)S(1)} %get-tuple-element.38.refs_3_), custom_call_target="tpu_custom_call" | custom-call | tf_op jit(solution)/shard_map/pallas_call | solution.py:650
Async XLA Ops:
  1.2 7.4 %collective-permute-start.3 = (bf16[2,16,2560]{2,1,0:T(8,128)(2,1)S(1)}, bf16[2,16,2560]{2,1,0:T(8,128)(2,1)S(1)}, u32[]{:S(2)}, u32[]{:S(2)}) collective-permute-start(bf16[2,16,2560]{2,1,0:T(8,128)(2,1)S(1)} %get-tuple-element.29), channel_id=1, source_target_pairs={{0,1},{1,0},{2,3},{3,2},{4,5},{5,4},{6,7},{7,6},{8,9},{9,8},{10,11... | collective-permute-start | bytes 491528 | tf_op jit(solution)/shard_map/ppermute | solution.py:584
  1.7 6.9 %collective-permute-start.1 = (bf16[2,32,128]{2,1,0:T(8,128)(2,1)S(1)}, bf16[2,32,128]{2,1,0:T(8,128)(2,1)S(1)}, u32[]{:S(2)}, u32[]{:S(2)}) collective-permute-start(bf16[2,32,128]{2,1,0:T(8,128)(2,1)S(1)} %get-tuple-element.27), channel_id=1, source_target_pairs={{0,2},{2,0},{1,3},{3,1},{4,6},{6,4},{5,7},{7,5},{8,10},{10,8},{9,1... | collective-permute-start | bytes 49160 | tf_op jit(solution)/shard_map/ppermute | solution.py:582
  4.3 4.3 %collective-permute-start.2 = (bf16[2,16,128]{2,1,0:T(8,128)(2,1)S(1)}, bf16[2,16,128]{2,1,0:T(8,128)(2,1)S(1)}, u32[]{:S(2)}, u32[]{:S(2)}) collective-permute-start(bf16[2,16,128]{2,1,0:T(8,128)(2,1)S(1)} %get-tuple-element.28), channel_id=1, source_target_pairs={{0,3},{1,2},{2,1},{3,0},{4,7},{5,6},{6,5},{7,4},{8,11},{9,10},{10,... | collective-permute-start | bytes 24584 | tf_op jit(solution)/shard_map/ppermute | solution.py:583
  4.7 9.4 %collective-permute-start = (bf16[128,128]{1,0:T(8,128)(2,1)S(1)}, bf16[128,128]{1,0:T(8,128)(2,1)S(1)}, u32[]{:S(2)}, u32[]{:S(2)}) collective-permute-start(bf16[128,128]{1,0:T(8,128)(2,1)S(1)} %shard_map.47), channel_id=1, source_target_pairs={{0,12},{4,8},{8,4},{12,0},{1,13},{5,9},{9,5},{13,1},{2,14},{6,10},... | collective-permute-start | bytes 98312 | tf_op jit(solution)/shard_map/ppermute | solution.py:587
  9.3 10.3 %collective-permute-start.5 = (bf16[352,128]{1,0:T(8,128)(2,1)S(1)}, bf16[352,128]{1,0:T(8,128)(2,1)S(1)}, u32[]{:S(2)}, u32[]{:S(2)}) collective-permute-start(bf16[352,128]{1,0:T(8,128)(2,1)S(1)} %get-tuple-element.32), channel_id=1, source_target_pairs={{0,8},{4,12},{8,0},{12,4},{1,9},{5,13},{9,1},{13,5},{2,10},{6,14},... | collective-permute-start | bytes 270344 | tf_op jit(solution)/shard_map/ppermute | solution.py:587
  12.0 6.4 %collective-permute-start.4 = (bf16[208,128]{1,0:T(8,128)(2,1)S(1)}, bf16[208,128]{1,0:T(8,128)(2,1)S(1)}, u32[]{:S(2)}, u32[]{:S(2)}) collective-permute-start(bf16[208,128]{1,0:T(8,128)(2,1)S(1)} %get-tuple-element.31), channel_id=1, source_target_pairs={{0,12},{4,8},{8,4},{12,0},{1,13},{5,9},{9,5},{13,1},{2,14},{6,10},... | collective-permute-start | bytes 159752 | tf_op jit(solution)/shard_map/ppermute | solution.py:587
  13.3 6.2 %collective-permute-start.6 = (bf16[336,128]{1,0:T(8,128)(2,1)S(1)}, bf16[336,128]{1,0:T(8,128)(2,1)S(1)}, u32[]{:S(2)}, u32[]{:S(2)}) collective-permute-start(bf16[336,128]{1,0:T(8,128)(2,1)S(1)} %get-tuple-element.33), channel_id=1, source_target_pairs={{0,4},{4,0},{8,12},{12,8},{1,5},{5,1},{9,13},{13,9},{2,6},{6,2},{1... | collective-permute-start | bytes 258056 | tf_op jit(solution)/shard_map/ppermute | solution.py:587
  21.1 5.5 %collective-permute-start.7 = (f32[8,256]{1,0:T(8,128)S(1)}, f32[8,256]{1,0:T(8,128)S(1)}, u32[]{:S(2)}, u32[]{:S(2)}) collective-permute-start(f32[8,256]{1,0:T(8,128)S(1)} %get-tuple-element.35), channel_id=1, source_target_pairs={{0,12},{4,8},{8,4},{12,0},{1,13},{5,9},{9,5},{13,1},{2,14},{6,10},... | collective-permute-start | bytes 24584 | tf_op jit(solution)/shard_map/ppermute | solution.py:587
  23.7 4.5 %collective-permute-start.8 = (f32[8,256]{1,0:T(8,128)S(1)}, f32[8,256]{1,0:T(8,128)S(1)}, u32[]{:S(2)}, u32[]{:S(2)}) collective-permute-start(f32[8,256]{1,0:T(8,128)S(1)} %get-tuple-element.36), channel_id=1, source_target_pairs={{0,8},{4,12},{8,0},{12,4},{1,9},{5,13},{9,1},{13,5},{2,10},{6,14},... | collective-permute-start | bytes 24584 | tf_op jit(solution)/shard_map/ppermute | solution.py:587
  23.7 4.5 %collective-permute-start.9 = (f32[8,256]{1,0:T(8,128)S(1)}, f32[8,256]{1,0:T(8,128)S(1)}, u32[]{:S(2)}, u32[]{:S(2)}) collective-permute-start(f32[8,256]{1,0:T(8,128)S(1)} %get-tuple-element.37), channel_id=1, source_target_pairs={{0,4},{4,0},{8,12},{12,8},{1,5},{5,1},{9,13},{13,9},{2,6},{6,2},{1... | collective-permute-start | bytes 24584 | tf_op jit(solution)/shard_map/ppermute | solution.py:587
where the time goes:
time: 29.1 us; the launch traced here: 28.9 us
  starting transfers between devices  15 us (52%)
  Pallas kernels  7.06 us (24%)
  waiting for transfers between devices  6.82 us (23%)
    ppermute x7, starting transfers between devices, swapped(): return lax.ppermute(value, 'date', [(i, i ^ step) for i in range(dates)])  11.9 us
    ppermute x7, waiting for transfers between devices, swapped(): return lax.ppermute(value, 'date', [(i, i ^ step) for i in range(dates)])  6.81 us
    ppermute x1, starting transfers between devices, tiled_body(): side = lax.ppermute(side, 'rng', swap)  2.56 us
    pallas_call x1, Pallas kernels, tiled_body(): pl.pallas_call(functools.partial(looks_kernel, pairs, dates), out_shape=[...  1.58 us
    pallas_call x1, Pallas kernels, tiled_body(): pl.pallas_call(functools.partial(rest_kernel, tiles, others), out_shape=[...  1.35 us
    pallas_call x1, Pallas kernels, tiled_body(): pl.pallas_call(functools.partial(filter_kernel, pairs), out_shape=[jax.Sh...  1.23 us
    pallas_call x1, Pallas kernels, tiled_body(): pl.pallas_call(prepare_kernel, out_shape=[jax.ShapeDtypeStruct((2, lines,...  1.21 us
    pallas_call x1, Pallas kernels, tiled_body(): pl.pallas_call(functools.partial(place_kernel, min(LAGS, dates - 1), look...  0.73 us
  transfers between devices with their start and end apart: 10, of which 4 were waited for; matrix products, arithmetic and copies ran while one was open for 0% of the time, Pallas kernels for 12%

commit v1 on v0

--- a/solution.py
+++ b/solution.py
@@ -283,6 +283,10 @@
 TAIL = 2 * FILTER_HALF
 
 
+def reach(step, dates):
+    return {dates - 1: dates // 2, dates // 2: dates - 1}.get(step, step)
+
+
 def sinc(value):
     angle = jnp.pi * value
     return jnp.where(angle == 0.0, 1.0, jnp.sin(angle) / jnp.where(angle == 0.0, 1.0, angle))
@@ -314,8 +318,13 @@
         (slc_ref.at[:, :, outermost], side_ref),
         (slc_ref.at[:, nearest, outermost], corner_ref),
         (slc_ref.at[:, nearest, :], lines_ref),
-        (slc_ref, held_ref.at[:, :, pl.ds(LANES, columns)]),
     ]
+    for plane in range(2):
+        for part in range(lines // HALO_LINES):
+            for side in range(2):
+                at = pl.ds(part * HALO_LINES, HALO_LINES)
+                source = slc_ref.at[plane, at, pl.ds(side * columns // 2, columns // 2)]
+                moves.append((source, held_ref.at[plane, at, pl.ds(LANES + side * columns // 2, columns // 2)]))
     copies = [pltpu.make_async_copy(a, b, semaphores.at[i]) for i, (a, b) in enumerate(moves)]
     for copy in copies:
         copy.start()
@@ -330,9 +339,9 @@
         source = jnp.where(place < lines, place, place + jnp.where(az == 0, 0, -lines - HALO_LINES))
         taps = banded(tap_row(index_ref[0, 0]), source - line - offsets_ref[0, 0] + 3)
         line_ref[half] = jnp.concatenate(halves(taps), axis=0)
-    shape = (3 * LANES, LANES)
+    shape = (2 * LANES, LANES)
     distance = lax.broadcasted_iota(jnp.int32, shape, 0) - lax.broadcasted_iota(jnp.int32, shape, 1)
-    distance = distance - (LANES - FILTER_HALF - 3) - offsets_ref[0, 1]
+    distance = distance - (LANES // 2 - FILTER_HALF - 3) - offsets_ref[0, 1]
     taps = banded(tap_row(index_ref[0, 1]), distance)
     column_ref[...] = jnp.concatenate(halves(taps), axis=1)
     for copy in copies[2:]:
@@ -340,10 +349,10 @@
 
 
 def along_range(moved, column_ref, tiles):
-    high, low = halves(moved)
+    high, low = halves(pltpu.roll(moved, moved.shape[1] - LANES // 2, 1))
     starts = range(0, tiles * LANES, LANES)
-    high = jnp.concatenate([high[:, s : s + 3 * LANES] for s in starts], axis=0)
-    low = jnp.concatenate([low[:, s : s + 3 * LANES] for s in starts], axis=0)
+    high = jnp.concatenate([high[:, s : s + 2 * LANES] for s in starts], axis=0)
+    low = jnp.concatenate([low[:, s : s + 2 * LANES] for s in starts], axis=0)
     total = dot(high, column_ref[...])
     return total[:, :LANES] + total[:, LANES:] + dot(low, column_ref[:, :LANES])
 
@@ -351,7 +360,8 @@
 def early_kernel(tiles, held_ref, line_ref, column_ref, out_ref):
     lines = held_ref.shape[1]
     early = out_ref.shape[0] // (2 * HALO_LINES)
-    chunk = lax.axis_index("date") ^ (lax.axis_size("date") - 1)
+    dates = lax.axis_size("date")
+    chunk = lax.axis_index("date") ^ reach(dates - 1, dates)
     begin = pl.multiple_of((chunk * tiles + lax.axis_index("rng")) * LANES, LANES)
     moved = []
     for plane in range(2):
@@ -395,7 +405,7 @@
         wide_ref[plane, lines:, right : right + LANES] = jnp.where(block == 0, corner, zero[:HALO_LINES])
         wide_ref[plane, lines:, right + LANES :] = zero[:HALO_LINES]
     taps = jnp.concatenate([line_ref[0], line_ref[1]], axis=0)
-    chunk = lax.axis_index("date") ^ step
+    chunk = lax.axis_index("date") ^ reach(step, lax.axis_size("date"))
     read = pl.ds(pl.multiple_of(chunk * tiles * LANES, LANES), (tiles + 3) * LANES)
     moved = whole_lines(taps, [wide_ref[plane, :, read] for plane in range(2)])
     total = along_range(moved, column_ref, tiles + 1)
@@ -412,7 +422,8 @@
     taps = jnp.concatenate([line_ref[0], line_ref[1]], axis=0)
     rows = 2 * lines
     for step, out_ref in zip(steps, outs):
-        read = pl.ds(pl.multiple_of((date ^ step) * tiles * LANES, LANES), (tiles + 3) * LANES)
+        chunk = date ^ reach(step, lax.axis_size("date"))
+        read = pl.ds(pl.multiple_of(chunk * tiles * LANES, LANES), (tiles + 3) * LANES)
         moved = whole_lines(taps, [wide_ref[plane, :, read] for plane in range(2)])
         total = along_range(moved, column_ref, tiles + 1)
         tail = folded_tail(total[tiles * rows :])
@@ -443,14 +454,15 @@
     window = jnp.where(jnp.abs(spacing) <= FILTER_HALF, window, 0.0)
     copy.wait()
     for place, (first, second) in enumerate(pairs):
-        gap = shift_ref[date ^ first] - shift_ref[date ^ second]
+        dates = shift_ref.shape[0]
+        gap = shift_ref[date ^ reach(first, dates)] - shift_ref[date ^ reach(second, dates)]
         angle = jnp.where(jnp.abs(spacing) <= FILTER_HALF, jnp.pi * gap * spacing, 0.0)
         for part, taps in enumerate((window * jnp.cos(angle), window * jnp.sin(angle))):
             spread = jnp.broadcast_to(taps, (LANES, 2 * LANES))
             spread = pltpu.roll(spread, 0, 1, stride=1, stride_axis=0)
             high, low = halves(spread)
-            out_ref[place, 0, part * LANES : (part + 1) * LANES, :] = high
-            out_ref[place, 1, part * LANES : (part + 1) * LANES, :] = low
+            out_ref[place, part * LANES : (part + 1) * LANES, : 2 * LANES] = high
+            out_ref[place, part * LANES : (part + 1) * LANES, 2 * LANES :] = low
 
 
 def looks_kernel(pairs, dates, weight_ref, *refs):
@@ -483,7 +495,8 @@
             window_ref[step, at, LANES:] = value.astype(jnp.bfloat16)
     for place, (first, second) in enumerate(pairs):
         def filtered(step):
-            total = dot_nt(window_ref[step], weight_ref[place, 0]) + dot_nt(window_ref[step], weight_ref[place, 1])
+            window = window_ref[step]
+            total = dot_nt(jnp.concatenate([window, window], axis=1), weight_ref[place])
             total = total.reshape(blocks, 2, 2, HALO_LINES, 2 * LANES)
             re, im = total[:, :, 0], total[:, :, 1]
             return re[..., :LANES], im[..., :LANES], re[..., LANES:], im[..., LANES:]
@@ -517,7 +530,7 @@
         for place, pair in enumerate(pairs):
             if step in pair:
                 other = pair[1] if pair[0] == step else pair[0]
-                lag = (date ^ other) - (date ^ step)
+                lag = (date ^ reach(other, dates)) - (date ^ reach(step, dates))
                 for part in range(2):
                     signed = -total[place, part] if part == 1 and pair[1] == step else total[place, part]
                     value = jnp.where(own_lane == (lag - 1) * 2 + part, signed, value)
@@ -566,7 +579,7 @@
             jax.ShapeDtypeStruct((2, HALO_LINES, LANES), bf16),
             jax.ShapeDtypeStruct((2, HALO_LINES, columns), bf16),
             jax.ShapeDtypeStruct((2, 2 * HALO_LINES, lines + HALO_LINES), bf16),
-            jax.ShapeDtypeStruct((3 * LANES, 2 * LANES), bf16),
+            jax.ShapeDtypeStruct((2 * LANES, 2 * LANES), bf16),
             jax.ShapeDtypeStruct((2, lines, columns + 3 * LANES), bf16),
         ],
         in_specs=[hbm] * 3,
@@ -574,7 +587,7 @@
         scratch_shapes=[
             pltpu.SMEM(offsets.shape, jnp.int32),
             pltpu.SMEM(kernel_index.shape, jnp.int32),
-            pltpu.SemaphoreType.DMA((6,)),
+            pltpu.SemaphoreType.DMA((5 + 4 * (lines // HALO_LINES),)),
         ],
         compiler_params=limit,
     )(offsets, kernel_index, cells)
@@ -583,10 +596,6 @@
     corner = lax.ppermute(corner, ("rng", "az"), [(0, 3), (1, 2), (2, 1), (3, 0)])
     halo_lines = lax.ppermute(halo_lines, "az", swap)
 
-    def swapped(value, step):
-        return lax.ppermute(value, "date", [(i, i ^ step) for i in range(dates)])
-
-    steps = range(dates - 1, 0, -1)
     early_rows = (tiles - 1) * lines
     early = pl.pallas_call(
         functools.partial(early_kernel, tiles),
@@ -594,8 +603,13 @@
         in_specs=[vmem] * 3,
         out_specs=vmem,
         compiler_params=limit,
+        cost_estimate=pl.CostEstimate(flops=2_500_000_000, bytes_accessed=0, transcendentals=0),
     )(held, line_taps, column_taps)
-    early = swapped(early, steps[0])
+    early = lax.ppermute(early, "date", [(i, i ^ reach(dates - 1, dates)) for i in range(dates)])
+    def swapped(value, step):
+        return lax.ppermute(value, "date", [(i, i ^ reach(step, dates)) for i in range(dates)])
+
+    steps = range(dates - 1, 0, -1)
     first, wide = pl.pallas_call(
         functools.partial(first_kernel, tiles, steps[1]),
         out_shape=[
@@ -617,7 +631,7 @@
         in_specs=[vmem] * 3,
         out_specs=[vmem] * (dates - 1),
         compiler_params=limit,
-        cost_estimate=pl.CostEstimate(flops=400_000_000, bytes_accessed=0, transcendentals=0),
+        cost_estimate=pl.CostEstimate(flops=250_000_000, bytes_accessed=0, transcendentals=0),
     )(wide, line_taps, column_taps)
     rest = [swapped(rows, step) if step else rows for rows, step in zip(rest, others)]
     chunks = [rest[0], first, *rest[1:]]
@@ -626,14 +640,14 @@
     weights, early = pl.pallas_call(
         functools.partial(filter_kernel, pairs),
         out_shape=[
-            jax.ShapeDtypeStruct((len(pairs), 2, 2 * LANES, 2 * LANES), bf16),
+            jax.ShapeDtypeStruct((len(pairs), 2 * LANES, 4 * LANES), bf16),
             jax.ShapeDtypeStruct((chunk_rows, LANES), bf16),
         ],
         in_specs=[hbm, vmem],
         out_specs=[vmem] * 2,
         scratch_shapes=[pltpu.SMEM(range_shift.shape, jnp.float32), pltpu.SemaphoreType.DMA],
         compiler_params=limit,
-        cost_estimate=pl.CostEstimate(flops=935_000_000, bytes_accessed=0, transcendentals=0),
+        cost_estimate=pl.CostEstimate(flops=800_000_000, bytes_accessed=0, transcendentals=0),
     )(range_shift, early)
     looked = pl.pallas_call(
         functools.partial(looks_kernel, pairs, dates),
@@ -647,13 +661,15 @@
         ],
         compiler_params=limit,
     )(weights, early, *chunks)
+    returned = [looked[0]] + [swapped(looked[step], step) for step in range(1, dates)]
+    returned = [returned[reach(distance, dates)] for distance in reversed(range(dates))]
     out = pl.pallas_call(
         functools.partial(place_kernel, min(LAGS, dates - 1), looks),
         out_shape=jax.ShapeDtypeStruct((2, LAGS, groups, looks * dates), jnp.float32),
         in_specs=[vmem] * dates,
         out_specs=vmem,
         compiler_params=limit,
-    )(*[swapped(looked[step], step) for step in steps], looked[0])
+    )(*returned)
     return out[:, None]
 
 

time: 29.1 us -> 27.7 us (0.952)
  waiting for transfers between devices: 6.82 us -> 5.61 us
    ppermute x1, starting transfers between devices: 0.07 us -> 2.44 us  [tiled_body(): lax.ppermute(corner, ('rng', 'az'), [(0, 3), (1, 2), (2, 1), (3, 0)])]
    ppermute x1, starting transfers between devices: 2.56 us -> 0.64 us  [tiled_body(): side = lax.ppermute(side, 'rng', swap)]
    ppermute x7, waiting for transfers between devices: 6.81 us -> 5.6 us  [the longest x6 5.6 us: swapped(): lax.ppermute(value, 'date', [(i, i ^ reach(step, dates)) for i in range(d...]
    ppermute x1, starting transfers between devices: 0.52 us -> 0.04 us  [tiled_body(): halo_lines = lax.ppermute(halo_lines, 'az', swap)]
  transfers between devices with their start and end apart: 10 -> 10, of which waited for: 4 -> 4; matrix products, arithmetic and copies ran while one was open for 0% -> 0% of each run, Pallas kernels for 12% -> 13%
where the time goes in v1:
time: 27.7 us; the launch traced here: 27.5 us
  starting transfers between devices  14.9 us (54%)
  Pallas kernels  6.98 us (25%)
  waiting for transfers between devices  5.61 us (20%)
    ppermute x6, starting transfers between devices, swapped(): lax.ppermute(value, 'date', [(i, i ^ reach(step, dates)) for i in range(d...  8.86 us
    ppermute x6, waiting for transfers between devices, swapped(): lax.ppermute(value, 'date', [(i, i ^ reach(step, dates)) for i in range(d...  5.6 us
    ppermute x1, starting transfers between devices, tiled_body(): lax.ppermute(early, 'date', [(i, i ^ reach(dates - 1, dates)) for i in ra...  2.91 us
    ppermute x1, starting transfers between devices, tiled_body(): lax.ppermute(corner, ('rng', 'az'), [(0, 3), (1, 2), (2, 1), (3, 0)])  2.44 us
    pallas_call x1, Pallas kernels, tiled_body(): pl.pallas_call(functools.partial(looks_kernel, pairs, dates), out_shape=[...  1.58 us
    pallas_call x1, Pallas kernels, tiled_body(): pl.pallas_call(functools.partial(rest_kernel, tiles, others), out_shape=[...  1.29 us
    pallas_call x1, Pallas kernels, tiled_body(): pl.pallas_call(functools.partial(filter_kernel, pairs), out_shape=[jax.Sh...  1.23 us
    pallas_call x1, Pallas kernels, tiled_body(): pl.pallas_call(prepare_kernel, out_shape=[jax.ShapeDtypeStruct((2, lines,...  1.16 us
  transfers between devices with their start and end apart: 10, of which 4 were waited for; matrix products, arithmetic and copies ran while one was open for 0% of the time, Pallas kernels for 13%

profile of v1, /device:TPU:0, one launch (start us, length us, event | category | flops | bytes accessed | tf_op | source)
XLA Modules:
  0.0 27.5 jit_solution(18218192755103922109)
XLA Ops:
  0.0 1.2 %shard_map.46 = (bf16[2,32,128]{2,1,0:T(8,128)(2,1)S(1)}, bf16[2,16,128]{2,1,0:T(8,128)(2,1)S(1)}, bf16[2,16,2560]{2,1,0:T(8,128)(2,1)S(1)}, bf16[2,32,48]{2,1,0...) custom-call(s32[1,2]{1,0:T(1,128)} %offsets_hbm.1, s32[1,2]{1,0:T(1,128)} %index_hbm.1, ...), custom_call_target="tpu_custom_call" | custom-call | tf_op jit(solution)/shard_map/pallas_call | solution.py:575
  1.2 2.4 %collective-permute-start.2 = (bf16[2,16,128]{2,1,0:T(8,128)(2,1)S(1)}, bf16[2,16,128]{2,1,0:T(8,128)(2,1)S(1)}, u32[]{:S(2)}, u32[]{:S(2)}) collective-permute-start(bf16[2,16,128]{2,1,0:T(8,128)(2,1)S(1)} %get-tuple-element.28), channel_id=1, source_target_pairs={{0,3},{1,2},{2,1},{3,0},{4,7},{5,6},{6,5},{7,4},{8,11},{9,10},{10,... | collective-permute-start | bytes 24584 | tf_op jit(solution)/shard_map/ppermute | solution.py:596
  3.6 0.6 %collective-permute-start.1 = (bf16[2,32,128]{2,1,0:T(8,128)(2,1)S(1)}, bf16[2,32,128]{2,1,0:T(8,128)(2,1)S(1)}, u32[]{:S(2)}, u32[]{:S(2)}) collective-permute-start(bf16[2,32,128]{2,1,0:T(8,128)(2,1)S(1)} %get-tuple-element.27), channel_id=1, source_target_pairs={{0,2},{2,0},{1,3},{3,1},{4,6},{6,4},{5,7},{7,5},{8,10},{10,8},{9,1... | collective-permute-start | bytes 49160 | tf_op jit(solution)/shard_map/ppermute | solution.py:595
  4.2 0.0 collective-permute-start.3
  4.3 0.4 %shard_map.47 = bf16[128,128]{1,0:T(8,128)(2,1)S(1)} custom-call(bf16[2,32,2944]{2,1,0:T(8,128)(2,1)S(1)} %get-tuple-element.22.held_ref, bf16[2,32,48]{2,1,0:T(8,128)(2,1)S(1)} %get-tuple-element.23.line_ref, bf16[256,256]{1,0:T(8,128)(2,1)S(1)} %get-tuple-element.24.column_ref), custom_call_target="tpu_custom_call" | custom-call | flops 2500000000 | tf_op jit(solution)/shard_map/pallas_call | solution.py:600
  4.7 2.9 %collective-permute-start = (bf16[128,128]{1,0:T(8,128)(2,1)S(1)}, bf16[128,128]{1,0:T(8,128)(2,1)S(1)}, u32[]{:S(2)}, u32[]{:S(2)}) collective-permute-start(bf16[128,128]{1,0:T(8,128)(2,1)S(1)} %shard_map.47), channel_id=1, source_target_pairs={{0,8},{4,12},{8,0},{12,4},{1,9},{5,13},{9,1},{13,5},{2,10},{6,14},... | collective-permute-start | bytes 98312 | tf_op jit(solution)/shard_map/ppermute | solution.py:608
  7.6 0.0 collective-permute-done.2.corner_ref
  7.6 0.0 collective-permute-done.1.side_ref
  7.6 0.0 collective-permute-done.3.lines_ref
  7.6 0.6 %shard_map.49 = (bf16[352,128]{1,0:T(8,128)(2,1)S(1)}, bf16[2,48,2944]{2,1,0:T(8,128)(2,1)S(1)}) custom-call(bf16[2,32,128]{2,1,0:T(8,128)(2,1)S(1)} %collective-permute-done.1.side_ref, bf16[2,16,128]{2,1,0:T(8,128)(2,1)S(1)} %collective-permute-done.2.corner_ref, bf16[2,16,2560]{2,1,0:T(8,128)(2,1)S(1)} %collective-permute-done.3.lines_ref, ...), custom_call_target="tpu_custom_call" | custom-call | tf_op jit(solution)/shard_map/pallas_call | solution.py:613
  8.2 3.4 %collective-permute-start.5 = (bf16[352,128]{1,0:T(8,128)(2,1)S(1)}, bf16[352,128]{1,0:T(8,128)(2,1)S(1)}, u32[]{:S(2)}, u32[]{:S(2)}) collective-permute-start(bf16[352,128]{1,0:T(8,128)(2,1)S(1)} %get-tuple-element.32), channel_id=1, source_target_pairs={{0,12},{4,8},{8,4},{12,0},{1,13},{5,9},{9,5},{13,1},{2,14},{6,10},... | collective-permute-start | bytes 270344 | tf_op jit(solution)/shard_map/ppermute | solution.py:610
  11.6 1.3 %shard_map.50 = (bf16[208,128]{1,0:T(8,128)(2,1)S(1)}, bf16[336,128]{1,0:T(8,128)(2,1)S(1)}, bf16[336,128]{1,0:T(8,128)(2,1)S(1)}) custom-call(bf16[2,48,2944]{2,1,0:T(8,128)(2,1)S(1)} %get-tuple-element.30.wide_ref, bf16[2,32,48]{2,1,0:T(8,128)(2,1)S(1)} %get-tuple-element.23.line_ref, bf16[256,256]{1,0:T(8,128)(2,1)S(1)} %get-tuple-element.24.column_ref), custom_call_target="tpu_custom_call" | custom-call | flops 250000000 | tf_op jit(solution)/shard_map/pallas_call | solution.py:625
  12.9 0.0 collective-permute-start.6
  12.9 1.0 %collective-permute-start.4 = (bf16[208,128]{1,0:T(8,128)(2,1)S(1)}, bf16[208,128]{1,0:T(8,128)(2,1)S(1)}, u32[]{:S(2)}, u32[]{:S(2)}) collective-permute-start(bf16[208,128]{1,0:T(8,128)(2,1)S(1)} %get-tuple-element.31), channel_id=1, source_target_pairs={{0,8},{4,12},{8,0},{12,4},{1,9},{5,13},{9,1},{13,5},{2,10},{6,14},... | collective-permute-start | bytes 159752 | tf_op jit(solution)/shard_map/ppermute | solution.py:610
  13.9 0.0 collective-permute-done.early_ref
  13.9 1.2 %shard_map.48 = (bf16[6,256,512]{2,1,0:T(8,128)(2,1)S(1)}, bf16[320,128]{1,0:T(8,128)(2,1)S(1)}) custom-call(f32[4]{0:T(128)} %shift_hbm.1, bf16[128,128]{1,0:T(8,128)(2,1)S(1)} %collective-permute-done.early_ref), custom_call_target="tpu_custom_call" | custom-call | flops 800000000 | tf_op jit(solution)/shard_map/pallas_call | solution.py:640
  15.2 2.8 %collective-permute-done.4.refs_1_ = bf16[208,128]{1,0:T(8,128)(2,1)S(1)} collective-permute-done((bf16[208,128]{1,0:T(8,128)(2,1)S(1)}, bf16[208,128]{1,0:T(8,128)(2,1)S(1)}, u32[]{:S(2)}, u32[]{:S(2)}) %collective-permute-start.4) | collective-permute-done | bytes 53280 | tf_op jit(solution)/shard_map/ppermute | solution.py:610
  18.0 0.0 collective-permute-done.6.refs_3_
  18.0 0.0 collective-permute-done.5.refs_2_
  18.0 1.6 %shard_map.51 = (f32[8,256]{1,0:T(8,128)S(1)}, f32[8,256]{1,0:T(8,128)S(1)}, f32[8,256]{1,0:T(8,128)S(1)}, f32[8,256]{1,0:T(8,128)S(1)}) custom-call(bf16[6,256,512]{2,1,0:T(8,128)(2,1)S(1)} %get-tuple-element.25.weight_ref, bf16[320,128]{1,0:T(8,128)(2,1)S(1)} %get-tuple-element.26.refs_0_, bf16[208,128]{1,0:T(8,128)(2,1)S(1)} %collective-permute-done.4.refs_1_, ...), custom_call_target="tpu_custom_call" | custom-call | tf_op jit(solution)/shard_map/pallas_call | solution.py:652
  19.6 2.6 %collective-permute-start.7 = (f32[8,256]{1,0:T(8,128)S(1)}, f32[8,256]{1,0:T(8,128)S(1)}, u32[]{:S(2)}, u32[]{:S(2)}) collective-permute-start(f32[8,256]{1,0:T(8,128)S(1)} %get-tuple-element.35), channel_id=1, source_target_pairs={{0,12},{4,8},{8,4},{12,0},{1,13},{5,9},{9,5},{13,1},{2,14},{6,10},... | collective-permute-start | bytes 24584 | tf_op jit(solution)/shard_map/ppermute | solution.py:610
  22.2 0.9 %collective-permute-start.8 = (f32[8,256]{1,0:T(8,128)S(1)}, f32[8,256]{1,0:T(8,128)S(1)}, u32[]{:S(2)}, u32[]{:S(2)}) collective-permute-start(f32[8,256]{1,0:T(8,128)S(1)} %get-tuple-element.36), channel_id=1, source_target_pairs={{0,8},{4,12},{8,0},{12,4},{1,9},{5,13},{9,1},{13,5},{2,10},{6,14},... | collective-permute-start | bytes 24584 | tf_op jit(solution)/shard_map/ppermute | solution.py:610
  23.1 1.0 %collective-permute-start.9 = (f32[8,256]{1,0:T(8,128)S(1)}, f32[8,256]{1,0:T(8,128)S(1)}, u32[]{:S(2)}, u32[]{:S(2)}) collective-permute-start(f32[8,256]{1,0:T(8,128)S(1)} %get-tuple-element.37), channel_id=1, source_target_pairs={{0,4},{4,0},{8,12},{12,8},{1,5},{5,1},{9,13},{13,9},{2,6},{6,2},{1... | collective-permute-start | bytes 24584 | tf_op jit(solution)/shard_map/ppermute | solution.py:610
  24.0 1.1 %collective-permute-done.7.refs_0_ = f32[8,256]{1,0:T(8,128)S(1)} collective-permute-done((f32[8,256]{1,0:T(8,128)S(1)}, f32[8,256]{1,0:T(8,128)S(1)}, u32[]{:S(2)}, u32[]{:S(2)}) %collective-permute-start.7) | collective-permute-done | bytes 8224 | tf_op jit(solution)/shard_map/ppermute | solution.py:610
  25.1 1.6 %collective-permute-done.8.refs_1_ = f32[8,256]{1,0:T(8,128)S(1)} collective-permute-done((f32[8,256]{1,0:T(8,128)S(1)}, f32[8,256]{1,0:T(8,128)S(1)}, u32[]{:S(2)}, u32[]{:S(2)}) %collective-permute-start.8) | collective-permute-done | bytes 8224 | tf_op jit(solution)/shard_map/ppermute | solution.py:610
  26.7 0.1 collective-permute-done.9.refs_2_
  26.8 0.7 %shard_map.52 = f32[2,8,8,128]{3,2,1,0:T(8,128)} custom-call(f32[8,256]{1,0:T(8,128)S(1)} %collective-permute-done.7.refs_0_, f32[8,256]{1,0:T(8,128)S(1)} %collective-permute-done.8.refs_1_, f32[8,256]{1,0:T(8,128)S(1)} %collective-permute-done.9.refs_2_, f32[8,256]{1,0:T(8,128)S(1)} %get-tuple-element.38.refs_3_), custom_call_target="tpu_custom_call" | custom-call | tf_op jit(solution)/shard_map/pallas_call | solution.py:666
Async XLA Ops:
  1.2 6.4 %collective-permute-start.2 = (bf16[2,16,128]{2,1,0:T(8,128)(2,1)S(1)}, bf16[2,16,128]{2,1,0:T(8,128)(2,1)S(1)}, u32[]{:S(2)}, u32[]{:S(2)}) collective-permute-start(bf16[2,16,128]{2,1,0:T(8,128)(2,1)S(1)} %get-tuple-element.28), channel_id=1, source_target_pairs={{0,3},{1,2},{2,1},{3,0},{4,7},{5,6},{6,5},{7,4},{8,11},{9,10},{10,... | collective-permute-start | bytes 24584 | tf_op jit(solution)/shard_map/ppermute | solution.py:596
  3.6 4.0 %collective-permute-start.1 = (bf16[2,32,128]{2,1,0:T(8,128)(2,1)S(1)}, bf16[2,32,128]{2,1,0:T(8,128)(2,1)S(1)}, u32[]{:S(2)}, u32[]{:S(2)}) collective-permute-start(bf16[2,32,128]{2,1,0:T(8,128)(2,1)S(1)} %get-tuple-element.27), channel_id=1, source_target_pairs={{0,2},{2,0},{1,3},{3,1},{4,6},{6,4},{5,7},{7,5},{8,10},{10,8},{9,1... | collective-permute-start | bytes 49160 | tf_op jit(solution)/shard_map/ppermute | solution.py:595
  4.2 3.3 %collective-permute-start.3 = (bf16[2,16,2560]{2,1,0:T(8,128)(2,1)S(1)}, bf16[2,16,2560]{2,1,0:T(8,128)(2,1)S(1)}, u32[]{:S(2)}, u32[]{:S(2)}) collective-permute-start(bf16[2,16,2560]{2,1,0:T(8,128)(2,1)S(1)} %get-tuple-element.29), channel_id=1, source_target_pairs={{0,1},{1,0},{2,3},{3,2},{4,5},{5,4},{6,7},{7,6},{8,9},{9,8},{10,11... | collective-permute-start | bytes 491528 | tf_op jit(solution)/shard_map/ppermute | solution.py:597
  4.7 9.2 %collective-permute-start = (bf16[128,128]{1,0:T(8,128)(2,1)S(1)}, bf16[128,128]{1,0:T(8,128)(2,1)S(1)}, u32[]{:S(2)}, u32[]{:S(2)}) collective-permute-start(bf16[128,128]{1,0:T(8,128)(2,1)S(1)} %shard_map.47), channel_id=1, source_target_pairs={{0,8},{4,12},{8,0},{12,4},{1,9},{5,13},{9,1},{13,5},{2,10},{6,14},... | collective-permute-start | bytes 98312 | tf_op jit(solution)/shard_map/ppermute | solution.py:608
  8.2 9.8 %collective-permute-start.5 = (bf16[352,128]{1,0:T(8,128)(2,1)S(1)}, bf16[352,128]{1,0:T(8,128)(2,1)S(1)}, u32[]{:S(2)}, u32[]{:S(2)}) collective-permute-start(bf16[352,128]{1,0:T(8,128)(2,1)S(1)} %get-tuple-element.32), channel_id=1, source_target_pairs={{0,12},{4,8},{8,4},{12,0},{1,13},{5,9},{9,5},{13,1},{2,14},{6,10},... | collective-permute-start | bytes 270344 | tf_op jit(solution)/shard_map/ppermute | solution.py:610
  12.9 5.1 %collective-permute-start.6 = (bf16[336,128]{1,0:T(8,128)(2,1)S(1)}, bf16[336,128]{1,0:T(8,128)(2,1)S(1)}, u32[]{:S(2)}, u32[]{:S(2)}) collective-permute-start(bf16[336,128]{1,0:T(8,128)(2,1)S(1)} %get-tuple-element.33), channel_id=1, source_target_pairs={{0,4},{4,0},{8,12},{12,8},{1,5},{5,1},{9,13},{13,9},{2,6},{6,2},{1... | collective-permute-start | bytes 258056 | tf_op jit(solution)/shard_map/ppermute | solution.py:610
  12.9 5.1 %collective-permute-start.4 = (bf16[208,128]{1,0:T(8,128)(2,1)S(1)}, bf16[208,128]{1,0:T(8,128)(2,1)S(1)}, u32[]{:S(2)}, u32[]{:S(2)}) collective-permute-start(bf16[208,128]{1,0:T(8,128)(2,1)S(1)} %get-tuple-element.31), channel_id=1, source_target_pairs={{0,8},{4,12},{8,0},{12,4},{1,9},{5,13},{9,1},{13,5},{2,10},{6,14},... | collective-permute-start | bytes 159752 | tf_op jit(solution)/shard_map/ppermute | solution.py:610
  19.6 5.5 %collective-permute-start.7 = (f32[8,256]{1,0:T(8,128)S(1)}, f32[8,256]{1,0:T(8,128)S(1)}, u32[]{:S(2)}, u32[]{:S(2)}) collective-permute-start(f32[8,256]{1,0:T(8,128)S(1)} %get-tuple-element.35), channel_id=1, source_target_pairs={{0,12},{4,8},{8,4},{12,0},{1,13},{5,9},{9,5},{13,1},{2,14},{6,10},... | collective-permute-start | bytes 24584 | tf_op jit(solution)/shard_map/ppermute | solution.py:610
  22.2 4.6 %collective-permute-start.8 = (f32[8,256]{1,0:T(8,128)S(1)}, f32[8,256]{1,0:T(8,128)S(1)}, u32[]{:S(2)}, u32[]{:S(2)}) collective-permute-start(f32[8,256]{1,0:T(8,128)S(1)} %get-tuple-element.36), channel_id=1, source_target_pairs={{0,8},{4,12},{8,0},{12,4},{1,9},{5,13},{9,1},{13,5},{2,10},{6,14},... | collective-permute-start | bytes 24584 | tf_op jit(solution)/shard_map/ppermute | solution.py:610
  23.1 3.7 %collective-permute-start.9 = (f32[8,256]{1,0:T(8,128)S(1)}, f32[8,256]{1,0:T(8,128)S(1)}, u32[]{:S(2)}, u32[]{:S(2)}) collective-permute-start(f32[8,256]{1,0:T(8,128)S(1)} %get-tuple-element.37), channel_id=1, source_target_pairs={{0,4},{4,0},{8,12},{12,8},{1,5},{5,1},{9,13},{13,9},{2,6},{6,2},{1... | collective-permute-start | bytes 24584 | tf_op jit(solution)/shard_map/ppermute | solution.py:610
